TPU v7x, 256 devices: a whole 4x4x8 slice. The times are simulated.
256 devices in a mesh: half: 2 (over y_lo), row: 8 (over z), col: 16 (over y_hi, x, core).
Axes of the slice: x: 4, y: 4 (y_hi: 2, y_lo: 2; y = y_hi * 2 + y_lo), z: 8, core: 2. Of those that a mesh axis runs over, the one named last changes fastest.
Arguments:
- front: float32 [16384, 16384], P('row', ('col', 'half')), may hold values from -6 to 6
- children: float32 [2, 8192, 8192], P('half', 'row', 'col'), may hold values from -6 to 6
- child_map: int32 [2, 64], replicated, may hold values from 0 to 127, as said below
- inverses: float32 [2, 512, 512], replicated, as said below
Outputs:
- factored: float32 [16384, 16384], P('row', ('col', 'half'))
Inputs may be any that keep to these rules, and one draw needn't show every extreme that they name: child_map[c, k] is 2 k or 2 k + 1: each child covers one tile of every pair of parent tiles. `inverses`: upper triangular, entries on and above the diagonal independent.
All inputs are finite; a program needn't handle non-finite values.
Results may differ from a plain program's by a relative error of at most 0.0001.
Values sent between devices are 32-bit elements; how exact they have to be, the bound alone decides.
A program may use at most 128 MiB of HBM per device.

v0:
```python
import jax
import jax.numpy as jnp
from jax import lax
from jax.sharding import PartitionSpec as P

TILE = 128
PW = 512
PANELS = 2


def broadcast(value, axis, source):
    kept = jnp.where(lax.axis_index(axis) == source, value, 0).astype(value.dtype)
    return lax.psum(kept, axis)


def spread_rows(data, bits):
    count, width = data.shape
    tiles = data.reshape(count // TILE, 1, TILE, width)
    slots = jnp.arange(2, dtype=jnp.int32)
    picked = bits[:, None, None, None] == slots[None, :, None, None]
    return jnp.where(picked, tiles, 0.0).reshape(2 * count, width)


def spread_cols(data, bits):
    count, width = data.shape
    tiles = data.reshape(count, width // TILE, 1, TILE)
    slots = jnp.arange(2, dtype=jnp.int32)
    picked = bits[None, :, None, None] == slots[None, None, :, None]
    return jnp.where(picked, tiles, 0.0).reshape(count, 2 * width)


def times_transposed(left, right):
    return lax.dot_general(
        left,
        right,
        (((1,), (1,)), ((), ())),
        precision=lax.Precision.HIGHEST,
        preferred_element_type=jnp.float32,
    )


def panel_step(slab, panel, inverse, global_rows, block_id, block_width):
    row_width = slab.shape[0]
    col_count = lax.axis_size("col")
    owner_block = panel * PW // block_width
    owner = owner_block % 2 * col_count + owner_block // 2
    limit = (panel + 1) * PW
    factor = jnp.dot(
        slab, inverse, precision=lax.Precision.HIGHEST, preferred_element_type=jnp.float32
    )
    factor = jnp.where((global_rows >= limit)[:, None], factor, 0.0)
    factor = broadcast(factor, ("half", "col"), owner)
    first_col = block_id * block_width
    piece = lax.dynamic_slice_in_dim(factor, first_col % row_width, block_width, 0)
    cross = broadcast(piece, "row", first_col // row_width)
    return (factor, cross)


def apply_panel(matrix, factor, cross, panel, global_rows, block_id, block_width):
    updated = matrix - times_transposed(factor, cross)
    offset = panel * PW % block_width
    is_owner = block_id * block_width + offset == panel * PW
    keep = (global_rows >= (panel + 1) * PW)[:, None] & is_owner
    return updated.at[:, offset : offset + PW].set(jnp.where(keep, factor, updated))


def local(front, children, child_map, inverses):
    row_width, block_width = front.shape
    row_pos = lax.axis_index("row")
    col_pos = lax.axis_index("col")
    half_pos = lax.axis_index("half")
    block_id = 2 * col_pos + half_pos
    received = lax.all_to_all(children[0], "half", split_axis=1, concat_axis=0, tiled=True)
    child_rows = received.shape[0] // 2
    row_tiles = child_rows // TILE
    col_tiles = received.shape[1] // TILE
    row_first = row_pos * row_tiles
    col_first = col_pos * (2 * col_tiles) + half_pos * col_tiles
    row_steps = jnp.arange(row_tiles, dtype=jnp.int32)
    col_steps = jnp.arange(col_tiles, dtype=jnp.int32)
    matrix = front
    for source in range(2):
        block = received[source * child_rows : (source + 1) * child_rows]
        table = child_map[source]
        row_bits = lax.dynamic_slice_in_dim(table, row_first, row_tiles, 0) - 2 * (
            row_first + row_steps
        )
        col_bits = lax.dynamic_slice_in_dim(table, col_first, col_tiles, 0) - 2 * (
            col_first + col_steps
        )
        matrix = matrix + spread_cols(spread_rows(block, row_bits), col_bits)
    global_rows = row_pos * row_width + jnp.arange(row_width, dtype=jnp.int32)
    factors = panel_step(matrix, 0, inverses[0], global_rows, block_id, block_width)
    for panel in range(PANELS):
        factor, cross = factors
        later = panel + 1
        matrix = apply_panel(matrix, factor, cross, panel, global_rows, block_id, block_width)
        if later < PANELS:
            factors = panel_step(matrix, later, inverses[later], global_rows, block_id, block_width)
    return matrix


def solution(mesh):
    return jax.shard_map(
        local,
        mesh=mesh,
        in_specs=(P("row", ("col", "half")), P("half", "row", "col"), P(), P()),
        out_specs=P("row", ("col", "half")),
        check_vma=False,
    )
```

profile of v0, /device:TPU:36, one launch (start us, length us, event | category | flops | bytes accessed | tf_op | source)
XLA Modules:
  0.0 539.3 jit_solution(4581915311588746388)
XLA Ops:
  6.5 1.9 copy.5
  8.5 0.0 copy-start.3
  8.5 1.8 copy.6
  10.3 3.8 all-to-all-start
  14.1 0.0 all-reduce.5.cloned.1.call-start
  14.1 0.0 copy-done.3
  14.1 0.1 fusion.7
  14.2 0.1 iota_compare_fusion.3
  14.3 0.1 broadcast_in_dim.143
  14.4 0.1 iota_compare_fusion.2
  14.5 0.1 broadcast_in_dim.156
  14.6 0.1 fusion.9
  14.6 0.1 iota_compare_fusion.1
  14.7 0.1 broadcast_in_dim.146
  14.8 0.1 iota_compare_fusion
  14.9 0.1 broadcast_in_dim.159
  15.0 24.1 %all-to-all-done = f32[1024,2,256]{2,0,1:T(8,128)S(1)} async-done(((f32[1024,2,256]{2,0,1:T(8,128)}), f32[1024,2,256]{2,0,1:T(8,128)S(1)}, u32[]{:S(2)}, u32[]{:S(2)}) %all-to-all-start) | async-done | bytes 2097184 | tf_op jit(solution)/shard_map/all_to_all | solution.py:73
  39.2 0.1 fusion.14
  39.3 1.5 broadcast_in_dim.150
  40.8 2.3 broadcast_in_dim.151
  43.1 7.5 %broadcast_select_fusion.1 = f32[2048,2,128]{2,1,0:T(2,128)S(1)} fusion(f32[2048,2,128]{2,1,0:T(2,128)S(1)} %broadcast_in_dim.151, pred[2048]{0:T(1024)(128)(4,1)S(1)} %broadcast_in_dim.147), kind=kLoop, calls=%fused_computation.6 | loop fusion | flops 524288 | bytes 4196352 | tf_op jit(solution)/shard_map/jit(_where)/select_n | solution.py:21
  50.6 3.1 broadcast_in_dim.153
  53.6 6.5 %broadcast_in_dim.154 = f32[2048,512]{1,0:T(8,128)} reshape(f32[2048,2,2,128]{3,2,1,0:T(2,128)} %broadcast_in_dim.153) | data formatting | bytes 8388608 | tf_op jit(solution)/shard_map/jit(_where)/broadcast_in_dim | solution.py:29
  60.1 1.5 broadcast_in_dim.163
  61.6 2.3 broadcast_in_dim.164
  63.9 7.4 %broadcast_select_fusion = f32[2048,2,128]{2,1,0:T(2,128)S(1)} fusion(f32[2048,2,128]{2,1,0:T(2,128)S(1)} %broadcast_in_dim.164, pred[2048]{0:T(1024)(128)(4,1)S(1)} %broadcast_in_dim.160), kind=kLoop, calls=%fused_computation.5 | loop fusion | flops 524288 | bytes 4196352 | tf_op jit(solution)/shard_map/jit(_where)/select_n | solution.py:21
  71.4 3.1 broadcast_in_dim.165
  74.4 6.4 %broadcast_in_dim.166 = f32[2048,512]{1,0:T(8,128)} reshape(f32[2048,2,2,128]{3,2,1,0:T(2,128)} %broadcast_in_dim.165) | data formatting | bytes 8388608 | tf_op jit(solution)/shard_map/jit(_where)/broadcast_in_dim | solution.py:29
  80.9 6.4 %select_add_fusion = f32[2048,512]{1,0:T(8,128)S(1)} fusion(f32[2048,512]{1,0:T(8,128)} %broadcast_in_dim.166, f32[2048,512]{1,0:T(8,128)} %param.12, f32[2048,512]{1,0:T(8,128)} %broadcast_in_dim.154, pred[512]{0:T(512)(128)(4,1)S(1)} %broadcast_in_dim.157, pred[512]{0:T(512)(128)(4,1)S(1)} %broadcast_in_dim.144), kind=kLoop, calls=%fused_computation.4 | loop fusion | flops 4194304 | bytes 16778240 | tf_op jit(solution)/shard_map/add | solution.py:91
  87.3 2.0 copy-done
  89.2 8.2 %select_select_fusion.1 = f32[2048,512]{1,0:T(8,128)} fusion(f32[2048,512]{1,0:T(8,128)S(1)} %select_add_fusion, pred[2048]{0:T(1024)(128)(4,1)S(1)} %fusion.4, pred[]{:T(512)S(6)} %eq.94, f32[2,512,512]{2,1,0:T(8,128)S(1)} %copy-done.2), kind=kOutput, calls=%fused_computation.3 | convolution fusion | flops 6444548096 | bytes 9439233 | tf_op jit(solution)/shard_map/dot_general | solution.py:48
  97.4 0.0 all-reduce.5.cloned.1.call-update
  97.5 0.0 all-reduce.7.cloned.1.call-start
  97.5 123.7 %all-reduce.5.cloned.1.call-done = f32[2048,512]{1,0:T(8,128)} async-done(((f32[2048,512]{1,0:T(8,128)}), f32[2048,512]{1,0:T(8,128)}) %all-reduce.5.cloned.1.call-update) | async-done | bytes 4194320 | tf_op jit(solution)/shard_map/psum | solution.py:13
  221.3 2.3 dynamic-slice_select_fusion.1
  223.5 0.0 all-reduce.7.cloned.1.call-update
  223.6 0.2 all-reduce.9.cloned.1.call-start
  223.8 75.9 %all-reduce.7.cloned.1.call-done = f32[512,512]{1,0:T(8,128)} async-done(((f32[512,512]{1,0:T(8,128)}), f32[512,512]{1,0:T(8,128)}) %all-reduce.7.cloned.1.call-update) | async-done | bytes 1048592 | tf_op jit(solution)/shard_map/psum | solution.py:13
  299.7 11.8 %subtract_select_fusion.1 = f32[2048,512]{1,0:T(8,128)S(1)} fusion(f32[2048,512]{1,0:T(8,128)} %all-reduce.5.cloned.1.call-done, f32[2048,512]{1,0:T(8,128)} %copy-done, f32[512,512]{1,0:T(8,128)} %all-reduce.7.cloned.1.call-done, pred[2048]{0:T(1024)(128)(4,1)S(1)} %get-tuple-element.54), kind=kOutput, calls=%fused_computation.2 | convolution fusion | flops 6444548096 | bytes 13633536 | tf_op jit(solution)/shard_map/dot_general | solution.py:33
  311.5 2.0 copy-done.1
  313.4 8.2 %select_select_fusion = f32[2048,512]{1,0:T(8,128)} fusion(f32[2048,512]{1,0:T(8,128)S(1)} %subtract_select_fusion.1, pred[2048]{0:T(1024)(128)(4,1)S(1)} %get-tuple-element.53, pred[]{:T(512)S(6)} %eq.92, f32[2,512,512]{2,1,0:T(8,128)S(1)} %copy-done.2), kind=kOutput, calls=%fused_computation.1 | convolution fusion | flops 6444548096 | bytes 9439233 | tf_op jit(solution)/shard_map/dot_general | solution.py:48
  321.7 0.0 all-reduce.9.cloned.1.call-update
  321.7 0.0 all-reduce.11.cloned.1.call-start
  321.7 120.0 %all-reduce.9.cloned.1.call-done = f32[2048,512]{1,0:T(8,128)} async-done(((f32[2048,512]{1,0:T(8,128)}), f32[2048,512]{1,0:T(8,128)}) %all-reduce.9.cloned.1.call-update) | async-done | bytes 4194320 | tf_op jit(solution)/shard_map/psum | solution.py:13
  441.7 2.3 dynamic-slice_select_fusion
  444.0 0.0 all-reduce.11.cloned.1.call-update
  444.0 76.0 %all-reduce.11.cloned.1.call-done = f32[512,512]{1,0:T(8,128)} async-done(((f32[512,512]{1,0:T(8,128)}), f32[512,512]{1,0:T(8,128)}) %all-reduce.11.cloned.1.call-update) | async-done | bytes 1048592 | tf_op jit(solution)/shard_map/psum | solution.py:13
  520.1 12.7 %subtract_select_fusion = f32[2048,512]{1,0:T(8,128)} fusion(f32[2048,512]{1,0:T(8,128)} %all-reduce.9.cloned.1.call-done, f32[2048,512]{1,0:T(8,128)} %copy-done.1, f32[512,512]{1,0:T(8,128)} %all-reduce.11.cloned.1.call-done, pred[2048]{0:T(1024)(128)(4,1)S(1)} %broadcast_and_fusion.1), kind=kOutput, calls=%fused_computation | convolution fusion | flops 6444548096 | bytes 13633536 | tf_op jit(solution)/shard_map/dot_general | solution.py:33
  (12 shorter events, 0.1 us)
Async XLA Ops:
  8.5 5.7 %copy-start.3 = (s32[2,64]{1,0:T(2,128)S(1)}, s32[2,64]{1,0:T(2,128)}, u32[]{:S(2)}) copy-start(s32[2,64]{1,0:T(2,128)} %param.14) | copy-start | bytes 1540
  10.3 28.9 %all-to-all-start = ((f32[1024,2,256]{2,0,1:T(8,128)}), f32[1024,2,256]{2,0,1:T(8,128)S(1)}, u32[]{:S(2)}, u32[]{:S(2)}) async-start(f32[1024,2,256]{2,0,1:T(8,128)} %copy.6), calls=%async_computation | async-start | bytes 4194304 | tf_op jit(solution)/shard_map/all_to_all | solution.py:73
  14.1 207.2 %all-reduce.5.cloned.1.call-start = ((), (), s32[]{:S(2)}) async-start(), calls=%async_computation.1 | async-start | bytes 8388608 | tf_op jit(solution)/shard_map/psum | solution.py:13
  80.9 8.3 %copy-start.2 = (f32[2,512,512]{2,1,0:T(8,128)S(1)}, f32[2,512,512]{2,1,0:T(8,128)}, u32[]{:S(2)}) copy-start(f32[2,512,512]{2,1,0:T(8,128)} %param.15) | copy-start | bytes 6291460
  87.2 2.0 copy-start
  97.5 202.2 %all-reduce.7.cloned.1.call-start = ((), (), s32[]{:S(2)}) async-start(), calls=%async_computation.2 | async-start | bytes 2097152 | tf_op jit(solution)/shard_map/psum | solution.py:13
  223.6 218.1 %all-reduce.9.cloned.1.call-start = ((), (), s32[]{:S(2)}) async-start(), calls=%async_computation.3 | async-start | bytes 8388608 | tf_op jit(solution)/shard_map/psum | solution.py:13
  311.5 2.0 copy-start.1
  321.7 198.4 %all-reduce.11.cloned.1.call-start = ((), (), s32[]{:S(2)}) async-start(), calls=%async_computation.4 | async-start | bytes 2097152 | tf_op jit(solution)/shard_map/psum | solution.py:13
Sparse Core Ops, SparseCore 0:
  97.6 123.6 all-reduce.4
  223.7 75.9 all-reduce.6
  321.8 119.8 all-reduce.8
  444.1 75.9 all-reduce.10
where the time goes:
time: 540 us; the launch traced here: 539 us
  waiting for transfers between devices  420 us (78%)
  matrix products  40.9 us (8%)
  local copies, waits for them, and re-layouts  34.8 us (6%)
  other arithmetic  26.3 us (5%)
  between operations  13.3 us (2%)
    psum x4, waiting for transfers between devices, broadcast(): return lax.psum(kept, axis)  396 us
    dot_general x2, matrix products, times_transposed(): lax.dot_general(left, right, (((1,), (1,)), ((), ())), precision=lax.Prec...  24.4 us
    all_to_all x1, waiting for transfers between devices, local(): lax.all_to_all(children[0], 'half', split_axis=1, concat_axis=0, tiled=True)  24.1 us
    broadcast_in_dim x8, local copies, waits for them, and re-layouts, spread_cols(): return jnp.where(picked, tiles, 0.0).reshape(count, 2 * width)  19.2 us
    dot_general x2, matrix products, panel_step(): jnp.dot(slab, inverse, precision=lax.Precision.HIGHEST, preferred_element...  16.4 us
    select_n x2, other arithmetic, spread_rows(): return jnp.where(picked, tiles, 0.0).reshape(2 * count, width)  14.9 us
  transfers between devices with their start and end apart: 5, of which 5 were waited for; matrix products, arithmetic and copies ran while one was open for 0% of the time, Pallas kernels for 0%

commit v1 on v0

v1 whole, which is shorter than its diff:
```python
import jax
import jax.numpy as jnp
from jax import lax
from jax.experimental import pallas as pl
from jax.experimental.pallas import tpu as pltpu
from jax.sharding import PartitionSpec as P

TILE = 128
PW = 512
ROWS = 2048
COLS = 512
CHILD_ROWS = 1024
HALF_COLS = 256
TILES = ROWS // TILE
ITEM = 32
TREES = 4
NZ = 8
RING_CHUNKS = 8
STEPS = 28
F32 = jnp.float32
BF16 = jnp.bfloat16


def split(value):
    high = value.astype(BF16)
    return high, (value - high.astype(F32)).astype(BF16)


def dot(left, right):
    return lax.dot_general(left, right, (((1,), (0,)), ((), ())), preferred_element_type=F32)


def dot3(left, right):
    (lh, ll), (rh, rl) = left, right
    return dot(lh, rh) + (dot(lh, rl) + dot(ll, rh))


def tile_of(chunk):
    return 8 * (chunk // 8) + (chunk // 2) % 4 + 4 * (1 - chunk % 2)


def kernel(
    map_ref,
    front_hbm,
    child_hbm,
    inv_hbm,
    out_hbm,
    front,
    own,
    got,
    inv,
    inv_hi,
    inv_lo,
    rows,
    cross,
    wide,
    y_hi,
    y_lo,
    out,
    load_sem,
    store_sem,
    child_send,
    child_recv,
    tree_send,
    tree_recv,
    feed_send,
    mate_send,
    mate_recv,
    ring_send,
    ring_recv,
    cross_send,
    cross_recv,
    wide_send,
    wide_recv,
    widemate_send,
    widemate_recv,
):
    half = lax.axis_index("half")
    z = lax.axis_index("row")
    col = lax.axis_index("col")
    core = col % 2
    x = (col // 2) % 4
    yh = col // 8
    y = 2 * yh + half
    block = 2 * col + half

    mate = {"col": col + 1 - 2 * core}
    other = {"half": 1 - half}
    near_x = {"col": col + 2 * (1 - 2 * (x % 2))}
    far_x = {"col": col + 2 * (3 - 2 * x)}
    far_y = {"half": 1 - half, "col": col + 8 * (1 - 2 * yh)}
    links = (other, near_x, far_y, far_x)
    up = {"row": (z + 1) % NZ}
    down = {"row": (z + NZ - 1) % NZ}

    def remote(src, dst, send, recv, device):
        return pltpu.make_async_remote_copy(
            src_ref=src,
            dst_ref=dst,
            send_sem=send,
            recv_sem=recv,
            device_id=device,
            device_id_type=pl.DeviceIdType.MESH,
        )

    def wait_for(ref, sem):
        pltpu.make_async_copy(ref, ref, sem).wait()

    bits = (((y + 1) // 2 + core) % 2, ((x + 1) // 2) % 2, yh, x // 2)
    root = (bits[0] + bits[1] + bits[2] + bits[3]) == 0
    depth = []
    forward = []
    for tree in range(TREES):
        turned = [bits[(tree + 1 + k) % 4] for k in range(4)]
        turned[3] = 1 - turned[3]
        weight = turned[0] + turned[1] + turned[2] + turned[3]
        depth.append(jnp.where(root, 0, 1 + weight))
        flags = [None] * 4
        for k in range(4):
            above = turned[k]
            for later in range(k + 1, 4):
                above = above + turned[later]
            flag = jnp.logical_and(jnp.logical_not(root), above == 0)
            if k == 3:
                flag = jnp.logical_or(root, jnp.logical_and(flag, weight > 0))
            flags[(tree + 1 + k) % 4] = flag
        forward.append(flags)

    owner = jnp.logical_and(jnp.logical_and(x == 0, core == 0), y < 2)
    feeder = jnp.logical_and(owner, half == 1)
    fed = jnp.logical_and(root, core == 1)
    seeded = jnp.logical_and(root, core == 0)

    loads = [
        pltpu.make_async_copy(front_hbm, front, load_sem.at[0]),
        pltpu.make_async_copy(
            child_hbm.at[0, :, pl.ds(pl.multiple_of(half * HALF_COLS, HALF_COLS), HALF_COLS)],
            own,
            load_sem.at[1],
        ),
        pltpu.make_async_copy(inv_hbm, inv, load_sem.at[2]),
    ]
    for load in loads:
        load.start()
    barrier = pltpu.get_barrier_semaphore()
    for device in (mate, up, down) + links:
        pl.semaphore_signal(barrier, inc=1, device_id=device, device_id_type=pl.DeviceIdType.MESH)
    pl.semaphore_wait(barrier, 7)

    def child_piece(piece):
        theirs = pl.ds(pl.multiple_of((1 - half) * HALF_COLS, HALF_COLS), HALF_COLS)
        lines = pl.ds(pl.multiple_of(piece * TILE, TILE), TILE)
        return remote(
            child_hbm.at[0, lines, theirs], got.at[lines], child_send, child_recv.at[piece], other
        )

    @pl.when(owner)
    def _():
        for piece in (2, 0, 3, 1, 6, 4, 7, 5):
            child_piece(piece).start()

    for load in loads:
        load.wait()
    for panel in range(2):
        high, low = split(inv[panel])
        inv_hi[panel] = high
        inv_lo[panel] = low

    def assemble(tile):
        pair = tile // 2
        lines = pl.ds(pl.multiple_of(tile * TILE, TILE), TILE)
        child_lines = pl.ds(pl.multiple_of(pair * TILE, TILE), TILE)
        row_tile = z * (TILES // 2) + pair
        parts = []
        for q in range(4):
            value = front[lines, pl.ds(q * TILE, TILE)]
            col_tile = 4 * col + 2 * half + q // 2
            for ref, which in ((own, half), (got, 1 - half)):
                row_bit = map_ref[which, row_tile] - 2 * row_tile
                col_bit = map_ref[which, col_tile] - 2 * col_tile
                hit = jnp.logical_and(row_bit == tile % 2, col_bit == q % 2)
                value = value + jnp.where(hit, ref[child_lines, pl.ds(q // 2 * TILE, TILE)], 0.0)
            parts.append(value)
        return jnp.concatenate(parts, axis=1)

    def step(t, carry):
        @pl.when(jnp.logical_and(owner, t < TILES))
        def _():
            tile = tile_of(t)

            @pl.when(t % 4 < 2)
            def _():
                piece = tile // 2
                wait_for(got.at[pl.ds(pl.multiple_of(piece * TILE, TILE), TILE)], child_recv.at[piece])

            slab = assemble(tile)
            factor = dot3(split(slab), (inv_hi[half], inv_lo[half]))
            keep = z * TILES + tile >= 4 * (half + 1)
            start = pl.multiple_of(tile * TILE, TILE)
            rows[half, pl.ds(start, TILE)] = jnp.where(keep, factor, 0.0)

            @pl.when(feeder)
            def _():
                for tree in range(TREES):
                    item = rows.at[1, pl.ds(start + ITEM * tree, ITEM)]
                    remote(item, item, feed_send, tree_recv.at[tree, t], mate).start()

        @pl.when(jnp.logical_and(jnp.logical_not(owner), jnp.logical_and(t % 2 == 0, t < 16)))
        def _():
            child_piece(t // 2).start()

        for tree in range(TREES):
            chunk = t - depth[tree]

            @pl.when(jnp.logical_and(chunk >= 0, chunk < TILES))
            def _():
                start = pl.multiple_of(tile_of(chunk) * TILE + ITEM * tree, ITEM)
                item = rows.at[core, pl.ds(start, ITEM)]

                @pl.when(jnp.logical_not(seeded))
                def _():
                    wait_for(item, tree_recv.at[tree, chunk])

                for link in range(4):

                    @pl.when(forward[tree][link])
                    def _():
                        remote(
                            item,
                            item,
                            tree_send.at[tree, link],
                            tree_recv.at[tree, chunk],
                            links[link],
                        ).start()

                @pl.when(jnp.logical_not(fed))
                def _():
                    remote(item, item, mate_send, mate_recv, mate).start()

        for tree in range(TREES):
            onward = up if tree < 2 else down
            hops = (z - 4 * yh - x + 2 * NZ) % NZ if tree < 2 else (4 * yh + x - z + NZ) % NZ
            late = t - (1 - half) - depth[tree] - hops
            chunk = late // 2

            @pl.when(
                jnp.logical_and(late >= 0, jnp.logical_and(late % 2 == 0, chunk < RING_CHUNKS))
            )
            def _():
                which = chunk // 4
                place = pl.multiple_of((chunk % 4) * TILE + ITEM * tree, ITEM)
                item = cross.at[which, pl.ds(place, ITEM)]

                @pl.when(hops == 0)
                def _():
                    tile = 8 * which + 4 * half + chunk % 4
                    start = pl.multiple_of(tile * TILE + ITEM * tree, ITEM)
                    cross[which, pl.ds(place, ITEM)] = rows[core, pl.ds(start, ITEM)]

                @pl.when(hops > 0)
                def _():
                    wait_for(item, ring_recv.at[tree, chunk])

                @pl.when(hops < NZ - 1)
                def _():
                    remote(
                        item, item, ring_send.at[tree], ring_recv.at[tree, chunk], onward
                    ).start()

                @pl.when(which != core)
                def _():
                    remote(
                        item, cross.at[2, pl.ds(place, ITEM)], cross_send, cross_recv, mate
                    ).start()

        for tree in range(TREES):
            onward = up if tree < 2 else down
            hops = z if tree < 2 else (NZ - z) % NZ
            late = t - depth[tree] - hops
            chunk = late // 2

            @pl.when(
                jnp.logical_and(
                    core == 0,
                    jnp.logical_and(late >= 0, jnp.logical_and(late % 2 == 0, chunk < 4)),
                )
            )
            def _():
                place = pl.multiple_of(chunk * TILE + ITEM * tree, ITEM)
                item = wide.at[pl.ds(place, ITEM)]

                @pl.when(hops == 0)
                def _():
                    wide[pl.ds(place, ITEM)] = rows[0, pl.ds(4 * TILE + place, ITEM)]

                @pl.when(hops > 0)
                def _():
                    wait_for(item, wide_recv.at[tree, chunk])

                @pl.when(hops < NZ - 1)
                def _():
                    remote(
                        item, item, wide_send.at[tree], wide_recv.at[tree, chunk], onward
                    ).start()

                remote(item, item, widemate_send, widemate_recv, mate).start()

        return carry

    lax.fori_loop(0, STEPS, step, 0)

    @pl.when(jnp.logical_not(feeder))
    def _():
        wait_for(rows.at[1 - core], mate_recv)

    wait_for(cross.at[2], cross_recv)

    @pl.when(core == 1)
    def _():
        wait_for(wide, widemate_recv)

    @pl.when(jnp.logical_not(owner))
    def _():
        for piece in range(8):
            wait_for(got.at[pl.ds(piece * TILE, TILE)], child_recv.at[piece])

    f0c_t = cross[jnp.where(core == 0, 0, 2)].T
    g1c_t = cross[jnp.where(core == 0, 2, 1)].T
    mixed_t = dot3(split(inv[1].T), split(wide[...]))
    mixed = mixed_t.T
    second = block == 1
    f1c_t = g1c_t - dot3(split(mixed_t), split(f0c_t))
    y0_t = jnp.where(second, mixed, f0c_t - dot3(split(mixed), split(f1c_t)))
    y1_t = jnp.where(second, 0.0, f1c_t)
    for index, value in ((0, y0_t), (1, y1_t), (2, f0c_t)):
        high, low = split(value)
        y_hi[index] = high
        y_lo[index] = low

    def update(tile, carry):
        lines = pl.ds(pl.multiple_of(tile * TILE, TILE), TILE)
        place = z * TILES + tile
        f0 = rows[0, lines]
        g1 = rows[1, lines]
        base = assemble(tile)
        base = jnp.where(jnp.logical_and(block == 0, place >= 4), f0, base)
        base = jnp.where(jnp.logical_and(second, place >= 8), g1, base)
        first = jnp.where(place < 8, 2, 0)
        total = dot3(split(f0), (y_hi[first], y_lo[first]))
        total = total + dot3(split(g1), (y_hi[1], y_lo[1]))
        out[lines] = base - total
        pltpu.make_async_copy(out.at[lines], out_hbm.at[lines], store_sem).start()
        return carry

    lax.fori_loop(0, TILES, update, 0)

    wait_for(out, store_sem)
    wait_for(got, child_send)

    @pl.when(feeder)
    def _():
        wait_for(rows.at[0], feed_send)

    @pl.when(jnp.logical_not(fed))
    def _():
        wait_for(rows.at[0], mate_send)

    wait_for(cross.at[0], cross_send)
    for tree in range(TREES):
        for link in range(4):

            @pl.when(forward[tree][link])
            def _():
                wait_for(rows.at[0, pl.ds(0, TILES * ITEM)], tree_send.at[tree, link])

        hops = (z - 4 * yh - x + 2 * NZ) % NZ if tree < 2 else (4 * yh + x - z + NZ) % NZ

        @pl.when(hops < NZ - 1)
        def _():
            wait_for(rows.at[0, pl.ds(0, RING_CHUNKS * ITEM)], ring_send.at[tree])

        hops = z if tree < 2 else (NZ - z) % NZ

        @pl.when(jnp.logical_and(core == 0, hops < NZ - 1))
        def _():
            wait_for(rows.at[0, pl.ds(0, 4 * ITEM)], wide_send.at[tree])

    @pl.when(core == 0)
    def _():
        wait_for(wide, widemate_send)


def local(front, children, child_map, inverses):
    hbm = pl.BlockSpec(memory_space=pl.ANY)
    dma = pltpu.SemaphoreType.DMA
    return pl.pallas_call(
        kernel,
        out_shape=jax.ShapeDtypeStruct((ROWS, COLS), F32),
        in_specs=[pl.BlockSpec(memory_space=pltpu.SMEM), hbm, hbm, hbm],
        out_specs=hbm,
        scratch_shapes=[
            pltpu.VMEM((ROWS, COLS), F32),
            pltpu.VMEM((CHILD_ROWS, HALF_COLS), F32),
            pltpu.VMEM((CHILD_ROWS, HALF_COLS), F32),
            pltpu.VMEM((2, PW, PW), F32),
            pltpu.VMEM((2, PW, PW), BF16),
            pltpu.VMEM((2, PW, PW), BF16),
            pltpu.VMEM((2, ROWS, PW), F32),
            pltpu.VMEM((3, PW, PW), F32),
            pltpu.VMEM((PW, PW), F32),
            pltpu.VMEM((3, PW, COLS), BF16),
            pltpu.VMEM((3, PW, COLS), BF16),
            pltpu.VMEM((ROWS, COLS), F32),
            dma((3,)),
            dma,
            dma,
            dma((8,)),
            dma((TREES, 4)),
            dma((TREES, TILES)),
            dma,
            dma,
            dma,
            dma((TREES,)),
            dma((TREES, RING_CHUNKS)),
            dma,
            dma,
            dma((TREES,)),
            dma((TREES, 4)),
            dma,
            dma,
        ],
        compiler_params=pltpu.CompilerParams(
            collective_id=0, has_side_effects=True, vmem_limit_bytes=56 * 1024 * 1024
        ),
    )(child_map, front, children, inverses)


def solution(mesh):
    return jax.shard_map(
        local,
        mesh=mesh,
        in_specs=(P("row", ("col", "half")), P("half", "row", "col"), P(), P()),
        out_specs=P("row", ("col", "half")),
        check_vma=False,
    )
```

time: 540 us -> 139 us (0.26)
  waiting for transfers between devices: 420 us -> 0 us
  Pallas kernels: 0 us -> 132 us
  matrix products: 40.9 us -> 0 us
  local copies, waits for them, and re-layouts: 34.8 us -> 4.64 us
  other arithmetic: 26.3 us -> 0 us
  between operations: 13.3 us -> 0.01 us
    psum x4 -> x0, waiting for transfers between devices: 396 us -> none  [broadcast(): return lax.psum(kept, axis)]
    pallas_call x0 -> x1, Pallas kernels: none -> 132 us  [local(): pl.pallas_call(kernel, out_shape=jax.ShapeDtypeStruct((ROWS, COLS), F32),...]
    dot_general x4 -> x0, matrix products: 40.9 us -> none  [the longest x2 24.4 us: times_transposed(): lax.dot_general(left, right, (((1,), (1,)), ((), ())), precision=lax.Prec...]
    broadcast_in_dim x16 -> x0, local copies, waits for them, and re-layouts: 27 us -> none  [the longest x8 19.2 us: spread_cols(): return jnp.where(picked, tiles, 0.0).reshape(count, 2 * width)]
    all_to_all x1 -> x0, waiting for transfers between devices: 24.1 us -> none  [local(): lax.all_to_all(children[0], 'half', split_axis=1, concat_axis=0, tiled=True)]
    select_n x4 -> x0, other arithmetic: 19.5 us -> none  [the longest x2 14.9 us: spread_rows(): return jnp.where(picked, tiles, 0.0).reshape(2 * count, width)]
    add x1 -> x0, other arithmetic: 6.37 us -> none  [local(): matrix = matrix + spread_cols(spread_rows(block, row_bits), col_bits)]
  transfers between devices with their start and end apart: 5 -> 0, of which waited for: 5 -> 0; matrix products, arithmetic and copies ran while one was open for 0% -> 0% of each run, Pallas kernels for 0% -> 0%
where the time goes in v1:
time: 139 us; the launch traced here: 137 us
  Pallas kernels  132 us (95%)
  local copies, waits for them, and re-layouts  4.64 us (3%)
    pallas_call x1, Pallas kernels, local(): pl.pallas_call(kernel, out_shape=jax.ShapeDtypeStruct((ROWS, COLS), F32),...  132 us
    unnamed x1, local copies, waits for them, and re-layouts  4.64 us

profile of v1, /device:TPU:36, one launch (start us, length us, event | category | flops | bytes accessed | tf_op | source)
XLA Modules:
  0.0 136.9 jit_solution(6898618284395061366)
XLA Ops:
  0.0 132.2 %shard_map.46 = f32[2048,512]{1,0:T(8,128)} custom-call(s32[2,64]{1,0:T(2,128)} %map_ref.1, f32[2048,512]{1,0:T(8,128)} %front_hbm.1, f32[1,1024,512]{2,1,0:T(8,128)} %child_hbm.1, f32[2,512,512]{2,1,0:T(8,128)} %inv_hbm.1), custom_call_target="tpu_custom_call" | custom-call | tf_op jit(solution)/shard_map/pallas_call | solution.py:396
  132.2 4.6 %copy.6 = f32[2048,512]{1,0:T(8,128)} copy(f32[2048,512]{1,0:T(8,128)} %shard_map.46) | data formatting | bytes 8388608

commit v2 on v1

v2 whole, which is shorter than its diff:
```python
import jax
import jax.numpy as jnp
from jax import lax
from jax.experimental import pallas as pl
from jax.experimental.pallas import tpu as pltpu
from jax.sharding import PartitionSpec as P

TILE = 128
PW = 512
ROWS = 2048
COLS = 512
CHILD_ROWS = 1024
HALF_COLS = 256
TILES = ROWS // TILE
ITEM = 32
PAIR = 2 * ITEM
TREES = 4
NZ = 8
RING_PIECES = 16
SLACK = 3
CHILD_STEP = 18
CHILD_PIECES = 32
LAST = 5 * SLACK
WIDE_STEP = 9 + 7 * SLACK
STEPS = TILES + 1 + 12 * SLACK
F32 = jnp.float32
BF16 = jnp.bfloat16


def split(value):
    high = value.astype(BF16)
    return high, (value - high.astype(F32)).astype(BF16)


def dot(left, right):
    return lax.dot_general(left, right, (((1,), (0,)), ((), ())), preferred_element_type=F32)


def stacked(value):
    high, low = split(value)
    return jnp.concatenate([high, low, high], axis=0)


def dot3(left, right):
    high, low = split(left)
    return dot(jnp.concatenate([high, high, low], axis=1), right)


def tile_of(chunk):
    pair = lax.div(chunk, 2)
    return 8 * lax.rem(pair, 2) + 4 - 4 * lax.rem(chunk, 2) + lax.div(chunk, 4)


def kernel(
    map_ref,
    front_hbm,
    child_hbm,
    inv_hbm,
    out_hbm,
    front,
    own,
    got,
    inv,
    inv3,
    rows,
    cross,
    wide,
    y3,
    out,
    load_sem,
    store_sem,
    child_send,
    child_recv,
    tree_send,
    tree_recv,
    feed_send,
    mate_send,
    mate_recv,
    ring_send,
    ring_recv,
    cross_send,
    cross_recv,
    climb_send,
    climb_recv,
    wide_send,
    wide_recv,
    widemate_send,
    widemate_recv,
):
    half = lax.axis_index("half")
    z = lax.axis_index("row")
    col = lax.axis_index("col")
    core = col % 2
    x = (col // 2) % 4
    yh = col // 8
    y = 2 * yh + half
    block = 2 * col + half

    mate = {"col": col + 1 - 2 * core}
    other = {"half": 1 - half}
    near_x = {"col": col + 2 * (1 - 2 * (x % 2))}
    far_x = {"col": col + 2 * (3 - 2 * x)}
    far_y = {"half": 1 - half, "col": col + 8 * (1 - 2 * yh)}
    links = (other, near_x, far_y, far_x)
    up = {"row": (z + 1) % NZ}
    down = {"row": (z + NZ - 1) % NZ}

    def remote(src, dst, send, recv, peer):
        return pltpu.make_async_remote_copy(
            src_ref=src,
            dst_ref=dst,
            send_sem=send,
            recv_sem=recv,
            device_id=peer,
            device_id_type=pl.DeviceIdType.MESH,
        )

    def wait_for(ref, sem):
        pltpu.make_async_copy(ref, ref, sem).wait()

    bits = (((y + 1) // 2 + core) % 2, ((x + 1) // 2) % 2, yh, x // 2)
    root = (bits[0] + bits[1] + bits[2] + bits[3]) == 0
    depth = []
    forward = []
    for tree in range(TREES):
        turned = [bits[(tree + 1 + k) % 4] for k in range(4)]
        turned[3] = 1 - turned[3]
        weight = turned[0] + turned[1] + turned[2] + turned[3]
        depth.append(jnp.where(root, 0, SLACK * (1 + weight)))
        flags = [None] * 4 + [jnp.logical_or(root, turned[3] == 0)]
        for k in range(4):
            above = turned[k]
            for later in range(k + 1, 4):
                above = above + turned[later]
            flag = jnp.logical_and(jnp.logical_not(root), above == 0)
            if k == 3:
                flag = jnp.logical_or(root, jnp.logical_and(flag, weight > 0))
            flags[(tree + 1 + k) % 4] = flag
        forward.append(flags)

    owner = jnp.logical_and(jnp.logical_and(x == 0, core == 0), y < 2)
    feeder = jnp.logical_and(owner, half == 1)
    fed = jnp.logical_and(root, core == 1)
    seeded = jnp.logical_and(root, core == 0)

    source = 4 * yh + x
    ring_hops = [(z - source + NZ) % NZ, (source - z + NZ) % NZ]
    wide_hops = [z, (NZ - z) % NZ]
    ring_start = [
        1 - half + jnp.maximum(depth[2 * way], depth[2 * way + 1]) + SLACK * ring_hops[way]
        for way in range(2)
    ]

    loads = [
        pltpu.make_async_copy(front_hbm, front, load_sem.at[0]),
        pltpu.make_async_copy(
            child_hbm.at[0, :, pl.ds(pl.multiple_of(half * HALF_COLS, HALF_COLS), HALF_COLS)],
            own,
            load_sem.at[1],
        ),
        pltpu.make_async_copy(inv_hbm, inv, load_sem.at[2]),
    ]
    for load in loads:
        load.start()
    barrier = pltpu.get_barrier_semaphore()
    for peer in (mate, up, down) + links:
        pl.semaphore_signal(barrier, inc=1, device_id=peer, device_id_type=pl.DeviceIdType.MESH)
    pl.semaphore_wait(barrier, 7)

    def child_piece(piece, count, recv):
        theirs = pl.ds(pl.multiple_of((1 - half) * HALF_COLS, HALF_COLS), HALF_COLS)
        lines = pl.ds(pl.multiple_of(piece * count, count), count)
        return remote(
            child_hbm.at[0, lines, theirs], got.at[lines], child_send, recv, other
        )

    @pl.when(owner)
    def _():
        for piece in (2, 0, 6, 4, 3, 1, 7, 5):
            child_piece(piece, TILE, child_recv.at[piece]).start()

    for load in loads:
        load.wait()
    for panel in range(2):
        inv3[panel] = stacked(inv[panel])

    def assemble(tile):
        pair = lax.div(tile, 2)
        lines = pl.ds(pl.multiple_of(tile * TILE, TILE), TILE)
        child_lines = pl.ds(pl.multiple_of(pair * TILE, TILE), TILE)
        row_tile = z * (TILES // 2) + pair
        parts = []
        for q in range(4):
            value = front[lines, pl.ds(q * TILE, TILE)]
            col_tile = 4 * col + 2 * half + q // 2
            for ref, which in ((own, half), (got, 1 - half)):
                row_bit = map_ref[which, row_tile] - 2 * row_tile
                col_bit = map_ref[which, col_tile] - 2 * col_tile
                hit = jnp.logical_and(row_bit == lax.rem(tile, 2), col_bit == q % 2)
                value = value + jnp.where(hit, ref[child_lines, pl.ds(q // 2 * TILE, TILE)], 0.0)
            parts.append(value)
        return jnp.concatenate(parts, axis=1)

    def spread(item, tree, send, recv):
        def give(link):
            @pl.when(forward[tree][link])
            def _():
                remote(item, item, send.at[tree, link], recv, links[link]).start()

        @pl.when(forward[tree][4])
        def _():
            give(tree)
            give((tree + 3) % 4)

            @pl.when(forward[tree][(tree + 2) % 4])
            def _():
                give((tree + 2) % 4)
                give((tree + 1) % 4)

    def step(t, carry):
        @pl.when(jnp.logical_and(owner, t < TILES))
        def _():
            tile = tile_of(t)

            @pl.when(lax.rem(t, 8) < 4)
            def _():
                piece = lax.div(tile, 2)
                wait_for(got.at[pl.ds(pl.multiple_of(piece * TILE, TILE), TILE)], child_recv.at[piece])

            slab = assemble(tile)
            factor = dot3(slab, inv3[half])
            keep = z * TILES + tile >= 4 * (half + 1)
            start = pl.multiple_of(tile * TILE, TILE)
            rows[half, pl.ds(start, TILE)] = jnp.where(keep, factor, 0.0)

            @pl.when(feeder)
            def _():
                for tree in range(TREES):
                    item = rows.at[1, pl.ds(start + ITEM * tree, ITEM)]
                    remote(item, item, feed_send, tree_recv.at[tree, t], mate).start()

        @pl.when(
            jnp.logical_and(
                jnp.logical_not(owner),
                jnp.logical_and(t >= CHILD_STEP, t < CHILD_STEP + CHILD_PIECES),
            )
        )
        def _():
            child_piece(t - CHILD_STEP, CHILD_ROWS // CHILD_PIECES, child_recv.at[0]).start()

        @pl.when(t < TILES + LAST)
        def _():
            for tree in range(TREES):
                chunk = t - depth[tree]

                @pl.when(jnp.logical_and(chunk >= 0, chunk < TILES))
                def _():
                    start = pl.multiple_of(tile_of(chunk) * TILE + ITEM * tree, ITEM)
                    item = rows.at[core, pl.ds(start, ITEM)]

                    @pl.when(jnp.logical_not(seeded))
                    def _():
                        wait_for(item, tree_recv.at[tree, chunk])

                    spread(item, tree, tree_send, tree_recv.at[tree, chunk])

            late = t - LAST

            @pl.when(jnp.logical_and(late >= 0, jnp.logical_not(fed)))
            def _():
                start = pl.multiple_of(tile_of(late) * TILE, TILE)
                item = rows.at[core, pl.ds(start, TILE)]
                remote(item, item, mate_send, mate_recv, mate).start()

        for way in range(2):
            onward = (up, down)[way]
            hops = ring_hops[way]
            piece = t - ring_start[way]

            @pl.when(jnp.logical_and(piece >= 0, piece < RING_PIECES))
            def _():
                which = lax.rem(lax.div(piece, 2), 2)
                place = lax.div(piece, 4) * TILE + PAIR * way + ITEM * lax.rem(piece, 2)
                place = pl.multiple_of(place, ITEM)
                item = cross.at[which, pl.ds(place, ITEM)]

                @pl.when(hops == 0)
                def _():
                    start = pl.multiple_of((8 * which + 4 * half) * TILE + place, ITEM)
                    cross[which, pl.ds(place, ITEM)] = rows[core, pl.ds(start, ITEM)]

                @pl.when(hops > 0)
                def _():
                    wait_for(item, ring_recv.at[way, piece])

                @pl.when(hops < NZ - 1)
                def _():
                    remote(
                        item, item, ring_send.at[way], ring_recv.at[way, piece], onward
                    ).start()

                @pl.when(which != core)
                def _():
                    remote(
                        item, cross.at[2, pl.ds(place, ITEM)], cross_send, cross_recv, mate
                    ).start()

        @pl.when(seeded)
        def _():
            for way in range(2):
                onward = (up, down)[way]
                hops = wide_hops[way]
                late = t - SLACK * hops
                chunk = lax.div(late, 4)

                @pl.when(jnp.logical_and(late >= 0, jnp.logical_and(lax.rem(late, 4) == 0, chunk < 4)))
                def _():
                    place = pl.multiple_of(chunk * TILE + PAIR * way, PAIR)
                    item = wide.at[pl.ds(place, PAIR)]

                    @pl.when(hops == 0)
                    def _():
                        wide[pl.ds(place, PAIR)] = rows[0, pl.ds(4 * TILE + place, PAIR)]

                    @pl.when(hops > 0)
                    def _():
                        wait_for(item, climb_recv.at[way, chunk])

                    @pl.when(hops < NZ - 1)
                    def _():
                        remote(
                            item, item, climb_send.at[way], climb_recv.at[way, chunk], onward
                        ).start()

        @pl.when(jnp.logical_and(core == 0, t >= WIDE_STEP))
        def _():
            for tree in range(TREES):
                part = t - WIDE_STEP - depth[tree]

                @pl.when(jnp.logical_and(part >= 0, part < 4))
                def _():
                    place = pl.multiple_of(part * TILE + ITEM * tree, ITEM)
                    item = wide.at[pl.ds(place, ITEM)]

                    @pl.when(jnp.logical_not(seeded))
                    def _():
                        wait_for(item, wide_recv.at[tree, part])

                    spread(item, tree, wide_send, wide_recv.at[tree, part])

            late = t - WIDE_STEP - LAST

            @pl.when(jnp.logical_and(late >= 0, late < 4))
            def _():
                item = wide.at[pl.ds(pl.multiple_of(late * TILE, TILE), TILE)]
                remote(item, item, widemate_send, widemate_recv, mate).start()

        return carry

    lax.fori_loop(0, STEPS, step, 0)

    @pl.when(jnp.logical_not(feeder))
    def _():
        wait_for(rows.at[1 - core], mate_recv)

    wait_for(cross.at[2], cross_recv)

    @pl.when(core == 1)
    def _():
        wait_for(wide, widemate_recv)

    @pl.when(jnp.logical_not(owner))
    def _():
        wait_for(got, child_recv.at[0])

    f0c_t = cross[jnp.where(core == 0, 0, 2)].T
    g1c_t = cross[jnp.where(core == 0, 2, 1)].T
    mixed_t = dot3(inv[1].T, stacked(wide[...]))
    mixed = mixed_t.T
    second = block == 1
    f1c_t = g1c_t - dot3(mixed_t, stacked(f0c_t))
    y0_t = jnp.where(second, mixed, f0c_t - dot3(mixed, stacked(f1c_t)))
    y1_t = jnp.where(second, 0.0, f1c_t)
    for index, value in ((0, y0_t), (1, y1_t), (2, f0c_t)):
        y3[index] = stacked(value)

    def update(tile, carry):
        lines = pl.ds(pl.multiple_of(tile * TILE, TILE), TILE)
        place = z * TILES + tile
        f0 = rows[0, lines]
        g1 = rows[1, lines]
        base = assemble(tile)
        base = jnp.where(jnp.logical_and(block == 0, place >= 4), f0, base)
        base = jnp.where(jnp.logical_and(second, place >= 8), g1, base)
        first = jnp.where(place < 8, 2, 0)
        total = dot3(f0, y3[first])
        total = total + dot3(g1, y3[1])
        out[lines] = base - total
        pltpu.make_async_copy(out.at[lines], out_hbm.at[lines], store_sem).start()
        return carry

    lax.fori_loop(0, TILES, update, 0)

    wait_for(out, store_sem)
    wait_for(got, child_send)

    @pl.when(feeder)
    def _():
        wait_for(rows.at[0], feed_send)

    @pl.when(jnp.logical_not(fed))
    def _():
        wait_for(rows.at[0], mate_send)

    wait_for(cross.at[0], cross_send)
    for tree in range(TREES):
        for link in range(4):

            @pl.when(forward[tree][link])
            def _():
                wait_for(rows.at[0, pl.ds(0, TILES * ITEM)], tree_send.at[tree, link])

                @pl.when(core == 0)
                def _():
                    wait_for(rows.at[0, pl.ds(0, 4 * ITEM)], wide_send.at[tree, link])

    for way in range(2):

        @pl.when(ring_hops[way] < NZ - 1)
        def _():
            wait_for(cross.at[0], ring_send.at[way])

        @pl.when(jnp.logical_and(seeded, wide_hops[way] < NZ - 1))
        def _():
            wait_for(rows.at[0, pl.ds(0, 4 * PAIR)], climb_send.at[way])

    @pl.when(core == 0)
    def _():
        wait_for(wide, widemate_send)


def local(front, children, child_map, inverses):
    hbm = pl.BlockSpec(memory_space=pl.ANY)
    dma = pltpu.SemaphoreType.DMA
    return pl.pallas_call(
        kernel,
        out_shape=jax.ShapeDtypeStruct((ROWS, COLS), F32),
        in_specs=[pl.BlockSpec(memory_space=pltpu.SMEM), hbm, hbm, hbm],
        out_specs=hbm,
        scratch_shapes=[
            pltpu.VMEM((ROWS, COLS), F32),
            pltpu.VMEM((CHILD_ROWS, HALF_COLS), F32),
            pltpu.VMEM((CHILD_ROWS, HALF_COLS), F32),
            pltpu.VMEM((2, PW, PW), F32),
            pltpu.VMEM((2, 3 * PW, PW), BF16),
            pltpu.VMEM((2, ROWS, PW), F32),
            pltpu.VMEM((3, PW, PW), F32),
            pltpu.VMEM((PW, PW), F32),
            pltpu.VMEM((3, 3 * PW, COLS), BF16),
            pltpu.VMEM((ROWS, COLS), F32),
            dma((3,)),
            dma,
            dma,
            dma((8,)),
            dma((TREES, 4)),
            dma((TREES, TILES)),
            dma,
            dma,
            dma,
            dma((2,)),
            dma((2, RING_PIECES)),
            dma,
            dma,
            dma((2,)),
            dma((2, 4)),
            dma((TREES, 4)),
            dma((TREES, 4)),
            dma,
            dma,
        ],
        compiler_params=pltpu.CompilerParams(
            collective_id=0, has_side_effects=True, vmem_limit_bytes=56 * 1024 * 1024
        ),
    )(child_map, front, children, inverses)


def solution(mesh):
    return jax.shard_map(
        local,
        mesh=mesh,
        in_specs=(P("row", ("col", "half")), P("half", "row", "col"), P(), P()),
        out_specs=P("row", ("col", "half")),
        check_vma=False,
    )
```

time: 139 us -> 109 us (0.78)
  Pallas kernels: 132 us -> 102 us
    pallas_call x1, Pallas kernels: 132 us -> 102 us  [local(): pl.pallas_call(kernel, out_shape=jax.ShapeDtypeStruct((ROWS, COLS), F32),...]
where the time goes in v2:
time: 109 us; the launch traced here: 107 us
  Pallas kernels  102 us (94%)
  local copies, waits for them, and re-layouts  4.64 us (4%)
    pallas_call x1, Pallas kernels, local(): pl.pallas_call(kernel, out_shape=jax.ShapeDtypeStruct((ROWS, COLS), F32),...  102 us
    unnamed x1, local copies, waits for them, and re-layouts  4.64 us

profile of v2, /device:TPU:36, one launch (start us, length us, event | category | flops | bytes accessed | tf_op | source)
XLA Modules:
  0.0 106.8 jit_solution(1340841385780593692)
XLA Ops:
  0.0 102.1 %shard_map.46 = f32[2048,512]{1,0:T(8,128)} custom-call(s32[2,64]{1,0:T(2,128)} %map_ref.1, f32[2048,512]{1,0:T(8,128)} %front_hbm.1, f32[1,1024,512]{2,1,0:T(8,128)} %child_hbm.1, f32[2,512,512]{2,1,0:T(8,128)} %inv_hbm.1), custom_call_target="tpu_custom_call" | custom-call | tf_op jit(solution)/shard_map/pallas_call | solution.py:445
  102.1 4.6 %copy.6 = f32[2048,512]{1,0:T(8,128)} copy(f32[2048,512]{1,0:T(8,128)} %shard_map.46) | data formatting | bytes 8388608

commit v3 on v2

--- a/solution.py
+++ b/solution.py
@@ -12,17 +12,20 @@
 CHILD_ROWS = 1024
 HALF_COLS = 256
 TILES = ROWS // TILE
+BIG = 256
 ITEM = 32
 PAIR = 2 * ITEM
 TREES = 4
 NZ = 8
-RING_PIECES = 16
+RING_PIECES = 20
+LONG_PIECES = 12
+NEAR_HOPS = (4, 3)
 SLACK = 3
-CHILD_STEP = 18
+CHILD_STEP = 17
 CHILD_PIECES = 32
 LAST = 5 * SLACK
-WIDE_STEP = 9 + 7 * SLACK
-STEPS = TILES + 1 + 12 * SLACK
+WIDE_STEP = 3 + 7 * SLACK
+STEPS = LAST + LONG_PIECES + 1 + 7 * SLACK
 F32 = jnp.float32
 BF16 = jnp.bfloat16
 
@@ -47,8 +50,7 @@
 
 
 def tile_of(chunk):
-    pair = lax.div(chunk, 2)
-    return 8 * lax.rem(pair, 2) + 4 - 4 * lax.rem(chunk, 2) + lax.div(chunk, 4)
+    return 8 * lax.div(chunk, 8) + 4 - 4 * lax.rem(chunk, 2) + lax.div(lax.rem(chunk, 8), 2)
 
 
 def kernel(
@@ -146,10 +148,8 @@
     source = 4 * yh + x
     ring_hops = [(z - source + NZ) % NZ, (source - z + NZ) % NZ]
     wide_hops = [z, (NZ - z) % NZ]
-    ring_start = [
-        1 - half + jnp.maximum(depth[2 * way], depth[2 * way + 1]) + SLACK * ring_hops[way]
-        for way in range(2)
-    ]
+    deepest = jnp.maximum(jnp.maximum(depth[0], depth[1]), jnp.maximum(depth[2], depth[3]))
+    ring_start = [1 - half + deepest + SLACK * hops for hops in ring_hops]
 
     loads = [
         pltpu.make_async_copy(front_hbm, front, load_sem.at[0]),
@@ -176,7 +176,7 @@
 
     @pl.when(owner)
     def _():
-        for piece in (2, 0, 6, 4, 3, 1, 7, 5):
+        for piece in (2, 0):
             child_piece(piece, TILE, child_recv.at[piece]).start()
 
     for load in loads:
@@ -222,7 +222,7 @@
         def _():
             tile = tile_of(t)
 
-            @pl.when(lax.rem(t, 8) < 4)
+            @pl.when(lax.rem(t, 4) < 2)
             def _():
                 piece = lax.div(tile, 2)
                 wait_for(got.at[pl.ds(pl.multiple_of(piece * TILE, TILE), TILE)], child_recv.at[piece])
@@ -264,6 +264,13 @@
 
                     spread(item, tree, tree_send, tree_recv.at[tree, chunk])
 
+            @pl.when(jnp.logical_and(owner, jnp.logical_and(lax.rem(t, 2) == 0, t < 12)))
+            def _():
+                count = lax.div(t, 2)
+                group = lax.div(count, 2) + 1
+                piece = 4 * lax.div(group, 2) + lax.rem(group, 2) + 2 - 2 * lax.rem(count, 2)
+                child_piece(piece, TILE, child_recv.at[piece]).start()
+
             late = t - LAST
 
             @pl.when(jnp.logical_and(late >= 0, jnp.logical_not(fed)))
@@ -276,34 +283,54 @@
             onward = (up, down)[way]
             hops = ring_hops[way]
             piece = t - ring_start[way]
-
-            @pl.when(jnp.logical_and(piece >= 0, piece < RING_PIECES))
-            def _():
-                which = lax.rem(lax.div(piece, 2), 2)
-                place = lax.div(piece, 4) * TILE + PAIR * way + ITEM * lax.rem(piece, 2)
-                place = pl.multiple_of(place, ITEM)
+            near = piece >= LONG_PIECES
+            reach = jnp.where(near, NEAR_HOPS[way], NZ - 1)
+
+            @pl.when(
+                jnp.logical_and(
+                    hops <= reach, jnp.logical_and(piece >= 0, piece < RING_PIECES)
+                )
+            )
+            def _():
+                rest = piece - LONG_PIECES
+                tile = jnp.where(near, 6 + lax.div(rest, 4), lax.div(piece, 2))
+                line = jnp.where(near, ITEM * lax.rem(rest, 4), PAIR * way + ITEM * lax.rem(piece, 2))
+                which = lax.div(tile, 4)
+                place = pl.multiple_of(lax.rem(tile, 4) * TILE + line, ITEM)
                 item = cross.at[which, pl.ds(place, ITEM)]
+
+                def pass_on(held, mine):
+                    @pl.when(hops < reach)
+                    def _():
+                        remote(
+                            held,
+                            item,
+                            ring_send.at[way, near.astype(jnp.int32)],
+                            ring_recv.at[way, piece],
+                            onward,
+                        ).start()
+
+                    @pl.when(jnp.logical_and(mine, which != core))
+                    def _():
+                        remote(
+                            held, cross.at[2, pl.ds(place, ITEM)], cross_send, cross_recv, mate
+                        ).start()
 
                 @pl.when(hops == 0)
                 def _():
                     start = pl.multiple_of((8 * which + 4 * half) * TILE + place, ITEM)
-                    cross[which, pl.ds(place, ITEM)] = rows[core, pl.ds(start, ITEM)]
+                    mine = piece < (RING_PIECES if way == 0 else LONG_PIECES)
+
+                    @pl.when(mine)
+                    def _():
+                        cross[which, pl.ds(place, ITEM)] = rows[core, pl.ds(start, ITEM)]
+
+                    pass_on(rows.at[core, pl.ds(start, ITEM)], mine)
 
                 @pl.when(hops > 0)
                 def _():
                     wait_for(item, ring_recv.at[way, piece])
-
-                @pl.when(hops < NZ - 1)
-                def _():
-                    remote(
-                        item, item, ring_send.at[way], ring_recv.at[way, piece], onward
-                    ).start()
-
-                @pl.when(which != core)
-                def _():
-                    remote(
-                        item, cross.at[2, pl.ds(place, ITEM)], cross_send, cross_recv, mate
-                    ).start()
+                    pass_on(item, True)
 
         @pl.when(seeded)
         def _():
@@ -311,9 +338,9 @@
                 onward = (up, down)[way]
                 hops = wide_hops[way]
                 late = t - SLACK * hops
-                chunk = lax.div(late, 4)
-
-                @pl.when(jnp.logical_and(late >= 0, jnp.logical_and(lax.rem(late, 4) == 0, chunk < 4)))
+                chunk = lax.div(late, 2)
+
+                @pl.when(jnp.logical_and(late >= 0, jnp.logical_and(lax.rem(late, 2) == 0, chunk < 4)))
                 def _():
                     place = pl.multiple_of(chunk * TILE + PAIR * way, PAIR)
                     item = wide.at[pl.ds(place, PAIR)]
@@ -384,22 +411,22 @@
     for index, value in ((0, y0_t), (1, y1_t), (2, f0c_t)):
         y3[index] = stacked(value)
 
-    def update(tile, carry):
-        lines = pl.ds(pl.multiple_of(tile * TILE, TILE), TILE)
-        place = z * TILES + tile
-        f0 = rows[0, lines]
-        g1 = rows[1, lines]
-        base = assemble(tile)
-        base = jnp.where(jnp.logical_and(block == 0, place >= 4), f0, base)
-        base = jnp.where(jnp.logical_and(second, place >= 8), g1, base)
-        first = jnp.where(place < 8, 2, 0)
-        total = dot3(f0, y3[first])
-        total = total + dot3(g1, y3[1])
-        out[lines] = base - total
-        pltpu.make_async_copy(out.at[lines], out_hbm.at[lines], store_sem).start()
+    def update(step, carry):
+        big = pl.ds(pl.multiple_of(step * BIG, BIG), BIG)
+        first = jnp.where(z * ROWS + step * BIG < 2 * PW, 2, 0)
+        out[big] = dot3(rows[0, big], y3[first]) + dot3(rows[1, big], y3[1])
+        for part in range(BIG // TILE):
+            tile = step * (BIG // TILE) + part
+            lines = pl.ds(pl.multiple_of(tile * TILE, TILE), TILE)
+            place = z * TILES + tile
+            base = assemble(tile)
+            base = jnp.where(jnp.logical_and(block == 0, place >= 4), rows[0, lines], base)
+            base = jnp.where(jnp.logical_and(second, place >= 8), rows[1, lines], base)
+            out[lines] = base - out[lines]
+        pltpu.make_async_copy(out.at[big], out_hbm.at[big], store_sem).start()
         return carry
 
-    lax.fori_loop(0, TILES, update, 0)
+    lax.fori_loop(0, ROWS // BIG, update, 0)
 
     wait_for(out, store_sem)
     wait_for(got, child_send)
@@ -428,7 +455,11 @@
 
         @pl.when(ring_hops[way] < NZ - 1)
         def _():
-            wait_for(cross.at[0], ring_send.at[way])
+            wait_for(rows.at[0, pl.ds(0, LONG_PIECES * ITEM)], ring_send.at[way, 0])
+
+        @pl.when(ring_hops[way] < NEAR_HOPS[way])
+        def _():
+            wait_for(rows.at[0, pl.ds(0, (RING_PIECES - LONG_PIECES) * ITEM)], ring_send.at[way, 1])
 
         @pl.when(jnp.logical_and(seeded, wide_hops[way] < NZ - 1))
         def _():
@@ -467,7 +498,7 @@
             dma,
             dma,
             dma,
-            dma((2,)),
+            dma((2, 2)),
             dma((2, RING_PIECES)),
             dma,
             dma,

time: 109 us -> 101 us (0.927); the launches traced: 107 us -> 101 us
  Pallas kernels: 102 us -> 95.9 us
    pallas_call x1, Pallas kernels: 102 us -> 95.9 us  [local(): pl.pallas_call(kernel, out_shape=jax.ShapeDtypeStruct((ROWS, COLS), F32),...]
where the time goes in v3:
time: 101 us
  Pallas kernels  95.9 us (95%)
  local copies, waits for them, and re-layouts  4.64 us (5%)
    pallas_call x1, Pallas kernels, local(): pl.pallas_call(kernel, out_shape=jax.ShapeDtypeStruct((ROWS, COLS), F32),...  95.9 us
    unnamed x1, local copies, waits for them, and re-layouts  4.64 us

profile of v3, /device:TPU:36, one launch (start us, length us, event | category | flops | bytes accessed | tf_op | source)
XLA Modules:
  0.0 100.5 jit_solution(16383832064051873762)
XLA Ops:
  0.0 95.9 %shard_map.46 = f32[2048,512]{1,0:T(8,128)} custom-call(s32[2,64]{1,0:T(2,128)} %map_ref.1, f32[2048,512]{1,0:T(8,128)} %front_hbm.1, f32[1,1024,512]{2,1,0:T(8,128)} %child_hbm.1, f32[2,512,512]{2,1,0:T(8,128)} %inv_hbm.1), custom_call_target="tpu_custom_call" | custom-call | tf_op jit(solution)/shard_map/pallas_call | solution.py:476
  95.9 4.6 %copy.6 = f32[2048,512]{1,0:T(8,128)} copy(f32[2048,512]{1,0:T(8,128)} %shard_map.46) | data formatting | bytes 8388608

commit v4 on v3

--- a/solution.py
+++ b/solution.py
@@ -23,6 +23,7 @@
 SLACK = 3
 CHILD_STEP = 17
 CHILD_PIECES = 32
+EARLY = 8
 LAST = 5 * SLACK
 WIDE_STEP = 3 + 7 * SLACK
 STEPS = LAST + LONG_PIECES + 1 + 7 * SLACK
@@ -179,10 +180,18 @@
         for piece in (2, 0):
             child_piece(piece, TILE, child_recv.at[piece]).start()
 
+    early = x > 0
+
+    @pl.when(early)
+    def _():
+        child_piece(0, EARLY * (CHILD_ROWS // CHILD_PIECES), child_recv.at[0]).start()
+
     for load in loads:
         load.wait()
-    for panel in range(2):
-        inv3[panel] = stacked(inv[panel])
+
+    @pl.when(owner)
+    def _():
+        inv3[...] = stacked(inv[half])
 
     def assemble(tile):
         pair = lax.div(tile, 2)
@@ -228,7 +237,7 @@
                 wait_for(got.at[pl.ds(pl.multiple_of(piece * TILE, TILE), TILE)], child_recv.at[piece])
 
             slab = assemble(tile)
-            factor = dot3(slab, inv3[half])
+            factor = dot3(slab, inv3[...])
             keep = z * TILES + tile >= 4 * (half + 1)
             start = pl.multiple_of(tile * TILE, TILE)
             rows[half, pl.ds(start, TILE)] = jnp.where(keep, factor, 0.0)
@@ -242,7 +251,9 @@
         @pl.when(
             jnp.logical_and(
                 jnp.logical_not(owner),
-                jnp.logical_and(t >= CHILD_STEP, t < CHILD_STEP + CHILD_PIECES),
+                jnp.logical_and(
+                    t >= CHILD_STEP + jnp.where(early, EARLY, 0), t < CHILD_STEP + CHILD_PIECES
+                ),
             )
         )
         def _():
@@ -483,7 +494,7 @@
             pltpu.VMEM((CHILD_ROWS, HALF_COLS), F32),
             pltpu.VMEM((CHILD_ROWS, HALF_COLS), F32),
             pltpu.VMEM((2, PW, PW), F32),
-            pltpu.VMEM((2, 3 * PW, PW), BF16),
+            pltpu.VMEM((3 * PW, PW), BF16),
             pltpu.VMEM((2, ROWS, PW), F32),
             pltpu.VMEM((3, PW, PW), F32),
             pltpu.VMEM((PW, PW), F32),

time: 101 us -> 97.9 us (0.969)
  Pallas kernels: 95.9 us -> 92.5 us
    pallas_call x1, Pallas kernels: 95.9 us -> 92.5 us  [local(): pl.pallas_call(kernel, out_shape=jax.ShapeDtypeStruct((ROWS, COLS), F32),...]
where the time goes in v4:
time: 97.9 us; the launch traced here: 97.2 us
  Pallas kernels  92.5 us (94%)
  local copies, waits for them, and re-layouts  4.64 us (5%)
    pallas_call x1, Pallas kernels, local(): pl.pallas_call(kernel, out_shape=jax.ShapeDtypeStruct((ROWS, COLS), F32),...  92.5 us
    unnamed x1, local copies, waits for them, and re-layouts  4.64 us

profile of v4, /device:TPU:36, one launch (start us, length us, event | category | flops | bytes accessed | tf_op | source)
XLA Modules:
  0.0 97.2 jit_solution(8534655323261980324)
XLA Ops:
  0.0 92.5 %shard_map.46 = f32[2048,512]{1,0:T(8,128)} custom-call(s32[2,64]{1,0:T(2,128)} %map_ref.1, f32[2048,512]{1,0:T(8,128)} %front_hbm.1, f32[1,1024,512]{2,1,0:T(8,128)} %child_hbm.1, f32[2,512,512]{2,1,0:T(8,128)} %inv_hbm.1), custom_call_target="tpu_custom_call" | custom-call | tf_op jit(solution)/shard_map/pallas_call | solution.py:487
  92.5 4.6 %copy.6 = f32[2048,512]{1,0:T(8,128)} copy(f32[2048,512]{1,0:T(8,128)} %shard_map.46) | data formatting | bytes 8388608

commit v5 on v4

--- a/solution.py
+++ b/solution.py
@@ -21,9 +21,9 @@
 LONG_PIECES = 12
 NEAR_HOPS = (4, 3)
 SLACK = 3
-CHILD_STEP = 17
+CHILD_STEP = 14
 CHILD_PIECES = 32
-EARLY = 8
+EARLY = 12
 LAST = 5 * SLACK
 WIDE_STEP = 3 + 7 * SLACK
 STEPS = LAST + LONG_PIECES + 1 + 7 * SLACK
@@ -180,7 +180,8 @@
         for piece in (2, 0):
             child_piece(piece, TILE, child_recv.at[piece]).start()
 
-    early = x > 0
+    early = jnp.logical_or(x > 0, y > 1)
+    child_step = jnp.where(early, CHILD_STEP - 4, CHILD_STEP)
 
     @pl.when(early)
     def _():
@@ -252,12 +253,12 @@
             jnp.logical_and(
                 jnp.logical_not(owner),
                 jnp.logical_and(
-                    t >= CHILD_STEP + jnp.where(early, EARLY, 0), t < CHILD_STEP + CHILD_PIECES
+                    t >= child_step + jnp.where(early, EARLY, 0), t < child_step + CHILD_PIECES
                 ),
             )
         )
         def _():
-            child_piece(t - CHILD_STEP, CHILD_ROWS // CHILD_PIECES, child_recv.at[0]).start()
+            child_piece(t - child_step, CHILD_ROWS // CHILD_PIECES, child_recv.at[0]).start()
 
         @pl.when(t < TILES + LAST)
         def _():

time: 97.9 us -> 96.2 us (0.983)
  the two profiles are of different devices: /device:TPU:36 before, /device:TPU:23 now
where the time goes in v5:
time: 96.2 us; the launch traced here: 96.1 us
  Pallas kernels  91.4 us (95%)
  local copies, waits for them, and re-layouts  4.64 us (5%)
    pallas_call x1, Pallas kernels, local(): pl.pallas_call(kernel, out_shape=jax.ShapeDtypeStruct((ROWS, COLS), F32),...  91.4 us
    unnamed x1, local copies, waits for them, and re-layouts  4.64 us

profile of v5, /device:TPU:23, one launch (start us, length us, event | category | flops | bytes accessed | tf_op | source)
XLA Modules:
  0.0 96.1 jit_solution(314592180965665167)
XLA Ops:
  0.0 91.4 %shard_map.46 = f32[2048,512]{1,0:T(8,128)} custom-call(s32[2,64]{1,0:T(2,128)} %map_ref.1, f32[2048,512]{1,0:T(8,128)} %front_hbm.1, f32[1,1024,512]{2,1,0:T(8,128)} %child_hbm.1, f32[2,512,512]{2,1,0:T(8,128)} %inv_hbm.1), custom_call_target="tpu_custom_call" | custom-call | tf_op jit(solution)/shard_map/pallas_call | solution.py:488
  91.4 4.6 %copy.6 = f32[2048,512]{1,0:T(8,128)} copy(f32[2048,512]{1,0:T(8,128)} %shard_map.46) | data formatting | bytes 8388608
